TPU v7x, 512 devices: a whole 4x8x8 slice. The times are simulated.
512 devices in a mesh: wide: 16 (over y, core), narrow: 32 (over z, x).
Axes of the slice: x: 4, y: 8, z: 8, core: 2. Of those that a mesh axis runs over, the one named last changes fastest.
Arguments:
- embeddings: bfloat16 [12288, 1024], P(('wide', 'narrow')), may hold values from -6 to 6
- cluster: int32 [512], replicated, may hold values from 0 to 44, never falling along the last dimension, each value on 1 to 34 neighbouring positions
Outputs:
- shifted: float32 [12288, 1024], P(('wide', 'narrow'))
Inputs may be any that keep to these rules, and one draw needn't show every extreme that they name: The blocks of one cluster are consecutive (ids never fall); each cluster holds 1 to 34 blocks, one exactly 34.
All inputs are finite; a program needn't handle non-finite values.
Results may differ from a plain program's by a relative error of at most 0.029.
Values may be sent and summed in bfloat16 or wider, within the bound.
A program may use at most 64 MiB of HBM per device.

v0:
```python
import math

import jax
import jax.numpy as jnp
from jax import lax
from jax.sharding import PartitionSpec as P

D = 1024
REACH = 2


SPREAD = 0.5


def from_behind(block, axis, distance):
    devices = range(lax.axis_size(axis))
    route = [(i - distance, i) for i in devices if i - distance in devices]
    return lax.ppermute(block, axis, route)


def normalize(rows):
    values = rows.astype(jnp.float32)
    factor = lax.rsqrt(jnp.mean(values * values, axis=1, keepdims=True) + 1e-06)
    return (values * factor).astype(jnp.bfloat16)


def tile_weights(group, keys, row_clusters, key_cluster, self_start):
    scores = lax.dot_general(
        group, keys, (((1,), (1,)), ((), ())), preferred_element_type=jnp.float32
    )
    weights = jnp.exp(scores * (1.0 / (SPREAD * math.sqrt(D))))
    keep = row_clusters[:, None] == key_cluster
    if self_start is not None:
        query_rows = lax.broadcasted_iota(jnp.int32, scores.shape, 0)
        key_rows = lax.broadcasted_iota(jnp.int32, scores.shape, 1) + self_start
        keep = keep & (query_rows != key_rows)
    return jnp.where(keep, weights, jnp.float32(0.0))


def on_device(embeddings, cluster):
    blk = embeddings.shape[0]
    n_narrow = lax.axis_size("narrow")
    n_wide = lax.axis_size("wide")
    wide_at = lax.axis_index("wide")
    narrow_at = lax.axis_index("narrow")
    normed = normalize(embeddings)
    group = lax.all_gather(normed, "narrow", axis=0, tiled=True)
    rows_all = group.shape[0]
    first_block = wide_at * n_narrow
    group_clusters = lax.dynamic_slice_in_dim(cluster, first_block, n_narrow)
    row_clusters = jnp.broadcast_to(group_clusters[:, None], (n_narrow, blk)).reshape(rows_all)
    own_block = first_block + narrow_at

    def block_cluster(offset):
        target = wide_at + offset
        inside = (target >= 0) & (target < n_wide)
        position = jnp.clip(own_block + offset * n_narrow, 0, cluster.shape[0] - 1)
        found = lax.dynamic_index_in_dim(cluster, position, 0, keepdims=False)
        return jnp.where(inside, found, -1)

    def forward(keys, key_cluster, self_start):
        weights = tile_weights(group, keys, row_clusters, key_cluster, self_start)
        added = jnp.dot(weights.astype(jnp.bfloat16), keys, preferred_element_type=jnp.float32)
        return (added, jnp.sum(weights, axis=1))

    numerator, total = forward(normed, block_cluster(0), narrow_at * blk)
    for offset in range(-REACH, REACH + 1):
        if offset != 0:
            keys = from_behind(normed, "wide", -offset)
            added, summed = forward(keys, block_cluster(offset), None)
            numerator = numerator + added
            total = total + summed
    own_numerator, own_total = (
        lax.psum_scatter(
            numerator.astype(jnp.bfloat16), "narrow", scatter_dimension=0, tiled=True
        ).astype(jnp.float32),
        lax.psum_scatter(
            total.astype(jnp.bfloat16), "narrow", scatter_dimension=0, tiled=True
        ).astype(jnp.float32),
    )
    return own_numerator / own_total[:, None]


def solution(mesh):
    in_specs = (P(("wide", "narrow"), None), P())
    out_specs = P(("wide", "narrow"), None)
    return jax.shard_map(
        on_device, mesh=mesh, in_specs=in_specs, out_specs=out_specs, check_vma=False
    )
```

profile of v0, /device:TPU:1, one launch (start us, length us, event | category | flops | bytes accessed | tf_op | source)
XLA Modules:
  0.0 330.1 jit_solution(4841747790055246149)
XLA Ops:
  6.5 0.0 all-gather.2.cloned.1.call-start
  6.5 0.9 fusion.10
  7.5 1.5 fusion.11
  9.0 0.0 copy-start.1
  9.0 0.0 all-gather.2.cloned.1.call-update
  9.0 0.0 reduce-scatter.2.cloned.1.call-start
  9.0 1.3 collective-permute-start.3
  10.3 8.8 %collective-permute-start.2 = (bf16[24,1024]{1,0:T(8,128)(2,1)}, bf16[24,1024]{1,0:T(8,128)(2,1)S(1)}, u32[]{:S(2)}, u32[]{:S(2)}) collective-permute-start(bf16[24,1024]{1,0:T(8,128)(2,1)} %fusion.11), channel_id=1, source_target_pairs={{32,0},{64,32},{96,64},{128,96},{160,128},{192,160},{224,192},{256... | collective-permute-start | bytes 147464 | tf_op jit(solution)/shard_map/ppermute | solution.py:18
  19.1 4.2 %collective-permute-start.1 = (bf16[24,1024]{1,0:T(8,128)(2,1)}, bf16[24,1024]{1,0:T(8,128)(2,1)S(1)}, u32[]{:S(2)}, u32[]{:S(2)}) collective-permute-start(bf16[24,1024]{1,0:T(8,128)(2,1)} %fusion.11), channel_id=1, source_target_pairs={{0,32},{32,64},{64,96},{96,128},{128,160},{160,192},{192,224},{224... | collective-permute-start | bytes 147464 | tf_op jit(solution)/shard_map/ppermute | solution.py:18
  23.3 2.0 collective-permute-start
  25.4 1.5 fusion.25
  30.0 0.8 broadcast_compare_fusion
  30.7 0.1 broadcast_in_dim.50
  30.8 0.1 eq.80
  30.9 0.1 broadcast_in_dim.56
  31.0 0.1 eq.89
  31.1 0.1 broadcast_in_dim.54
  31.2 0.1 eq.86
  31.3 0.1 broadcast_in_dim.52
  31.3 0.1 eq.83
  31.4 0.1 broadcast_in_dim.48
  31.5 0.1 eq.77
  31.6 63.9 %all-gather.2.cloned.1.call-done = bf16[768,1024]{1,0:T(8,128)(2,1)} async-done(((bf16[24,1024]{1,0:T(8,128)(2,1)}), bf16[768,1024]{1,0:T(8,128)(2,1)}) %all-gather.2.cloned.1.call-update) | async-done | bytes 1572880 | tf_op jit(solution)/shard_map/all_gather | solution.py:47
  95.6 2.0 fusion.29
  97.5 0.0 copy-done.1
  97.5 0.0 copy-start
  97.6 0.6 fusion.23
  98.1 0.0 collective-permute-done
  98.2 0.8 copy-done
  99.0 0.5 fusion.30
  99.5 0.6 fusion.21
  100.1 0.0 collective-permute-done.1
  100.1 0.5 fusion.28
  100.7 0.6 fusion.19
  101.3 0.0 collective-permute-done.2
  101.3 0.5 fusion.27
  101.8 0.6 fusion.17
  102.4 0.0 collective-permute-done.3
  102.4 0.5 fusion.26
  103.0 1.9 add_convert_fusion
  104.9 0.0 reduce-scatter.2.cloned.1.call-update
  104.9 1.3 dynamic-slice
  106.9 57.6 %all-reduce = bf16[768]{0:T(1024)(128)(2,1)S(1)} all-reduce(bf16[768]{0:T(1024)(128)(2,1)S(1)} %add_convert_fusion.1), channel_id=3, replica_groups=mesh['wide'=16,'narrow'=32] {'narrow'}, use_global_device_ids=true, to_apply=%region_7.8.clone | all-reduce | flops 768 | bytes 3072
  164.5 0.1 dynamic-slice_convert_fusion
  164.5 157.2 %reduce-scatter.2.cloned.1.call-done = bf16[24,1024]{1,0:T(8,128)(2,1)} async-done(((bf16[768,1024]{1,0:T(8,128)(2,1)}), bf16[24,1024]{1,0:T(8,128)(2,1)}) %reduce-scatter.2.cloned.1.call-update) | async-done | bytes 49168 | tf_op jit(solution)/shard_map/reduce_scatter | solution.py:74
  321.7 1.5 convert_divide_fusion
  (4 shorter events, 0.0 us)
Async XLA Ops:
  6.5 89.0 %all-gather.2.cloned.1.call-start = ((), (), s32[]{:S(2)}) async-start(), calls=%async_computation.1 | async-start | bytes 1622016 | tf_op jit(solution)/shard_map/all_gather | solution.py:47
  9.0 88.6 %copy-start.1 = (bf16[24,1024]{1,0:T(8,128)(2,1)S(1)}, bf16[24,1024]{1,0:T(8,128)(2,1)}, u32[]{:S(2)}) copy-start(bf16[24,1024]{1,0:T(8,128)(2,1)} %fusion.11) | copy-start | bytes 147460
  9.0 312.7 %reduce-scatter.2.cloned.1.call-start = ((), (), s32[]{:S(2)}) async-start(), calls=%async_computation.2 | async-start | bytes 1622016 | tf_op jit(solution)/shard_map/reduce_scatter | solution.py:74
  9.0 93.4 %collective-permute-start.3 = (bf16[24,1024]{1,0:T(8,128)(2,1)}, bf16[24,1024]{1,0:T(8,128)(2,1)S(1)}, u32[]{:S(2)}, u32[]{:S(2)}) collective-permute-start(bf16[24,1024]{1,0:T(8,128)(2,1)} %fusion.11), channel_id=1, source_target_pairs={{64,0},{96,32},{128,64},{160,96},{192,128},{224,160},{256,192},{28... | collective-permute-start | bytes 147464 | tf_op jit(solution)/shard_map/ppermute | solution.py:18
  10.3 90.9 %collective-permute-start.2 = (bf16[24,1024]{1,0:T(8,128)(2,1)}, bf16[24,1024]{1,0:T(8,128)(2,1)S(1)}, u32[]{:S(2)}, u32[]{:S(2)}) collective-permute-start(bf16[24,1024]{1,0:T(8,128)(2,1)} %fusion.11), channel_id=1, source_target_pairs={{32,0},{64,32},{96,64},{128,96},{160,128},{192,160},{224,192},{256... | collective-permute-start | bytes 147464 | tf_op jit(solution)/shard_map/ppermute | solution.py:18
  19.1 81.0 %collective-permute-start.1 = (bf16[24,1024]{1,0:T(8,128)(2,1)}, bf16[24,1024]{1,0:T(8,128)(2,1)S(1)}, u32[]{:S(2)}, u32[]{:S(2)}) collective-permute-start(bf16[24,1024]{1,0:T(8,128)(2,1)} %fusion.11), channel_id=1, source_target_pairs={{0,32},{32,64},{64,96},{96,128},{128,160},{160,192},{192,224},{224... | collective-permute-start | bytes 147464 | tf_op jit(solution)/shard_map/ppermute | solution.py:18
  23.3 74.8 %collective-permute-start = (bf16[24,1024]{1,0:T(8,128)(2,1)}, bf16[24,1024]{1,0:T(8,128)(2,1)S(1)}, u32[]{:S(2)}, u32[]{:S(2)}) collective-permute-start(bf16[24,1024]{1,0:T(8,128)(2,1)} %fusion.11), channel_id=1, source_target_pairs={{0,64},{32,96},{64,128},{96,160},{128,192},{160,224},{192,256},{22... | collective-permute-start | bytes 147464 | tf_op jit(solution)/shard_map/ppermute | solution.py:18
  97.5 1.4 copy-start
Sparse Core Ops, SparseCore 0:
  10.5 85.0 all-gather.1
  105.0 216.6 reduce-scatter.1
where the time goes:
time: 335 us; the launch traced here: 330 us
  waiting for transfers between devices  221 us (66%)
  blocking collectives  57.6 us (17%)
  between operations  17.3 us (5%)
  starting transfers between devices  16.3 us (5%)
  matrix products  8.42 us (3%)
  other arithmetic  4.81 us (1%)
  local copies, waits for them, and re-layouts  4.47 us (1%)
    reduce_scatter x1, waiting for transfers between devices, on_device(): lax.psum_scatter(numerator.astype(jnp.bfloat16), 'narrow', scatter_dimens...  157 us
    all_gather x1, waiting for transfers between devices, on_device(): group = lax.all_gather(normed, 'narrow', axis=0, tiled=True)  63.9 us
    unnamed x1, blocking collectives  57.6 us
    ppermute x4, starting transfers between devices, from_behind(): return lax.ppermute(block, axis, route)  16.3 us
  transfers between devices with their start and end apart: 6, of which 2 were waited for; matrix products, arithmetic and copies ran while one was open for 3% of the time, Pallas kernels for 0%

commit v1 on v0

v1 whole, which is shorter than its diff:
```python
import functools
import math

import jax
import jax.numpy as jnp
from jax import lax
from jax.experimental import pallas as pl
from jax.experimental.pallas import tpu as pltpu
from jax.sharding import PartitionSpec as P

D = 1024
BLK = 24
BLOCKS = 512
REACH = 33
SPREAD = 0.5
LANES = 128
MESH = pl.DeviceIdType.MESH

MARKS = (0, 27, 30, 29, 24, 12, 8, -2, -1, 1, 32)
COUNT = len(MARKS)
WIDTH = D + LANES


def pair_bits():
    bits = [0] * COUNT
    bits[0] |= 1
    for gap in range(1, REACH + 1):
        k, l = next(
            (k, l)
            for k in range(COUNT)
            for l in range(COUNT)
            if MARKS[l] - MARKS[k] == gap
        )
        bits[l] |= 1 << k
        bits[k] |= 1 << l
    return bits


def kernel(x_hbm, cluster_hbm, out_ref, raw, cluster, rows, parts, got, in_sem, send1, recv1, send2, recv2):
    n_narrow = lax.axis_size("narrow")
    me = lax.axis_index("wide") * n_narrow + lax.axis_index("narrow")

    def block_at(offset):
        return lax.rem(me + (offset % BLOCKS), BLOCKS)

    def device(offset):
        block = block_at(offset)
        return (lax.div(block, n_narrow), lax.rem(block, n_narrow))

    load = pltpu.make_async_copy(x_hbm, raw, in_sem.at[0])
    load.start()
    load_ids = pltpu.make_async_copy(cluster_hbm, cluster, in_sem.at[1])
    load_ids.start()

    barrier = pltpu.get_barrier_semaphore()
    for k in range(1, COUNT):
        pl.semaphore_signal(barrier, inc=1, device_id=device(MARKS[k]), device_id_type=MESH)

    load.wait()
    values = raw[...].astype(jnp.float32)
    factor = lax.rsqrt(jnp.mean(values * values, axis=1, keepdims=True) + 1e-06)
    rows[0, :, :D] = (values * factor).astype(jnp.bfloat16)
    rows[:, :, D:] = jnp.ones((COUNT, BLK, LANES), jnp.bfloat16)

    pl.semaphore_wait(barrier, COUNT - 1)
    gather = []
    for k in range(1, COUNT):
        copy = pltpu.make_async_remote_copy(
            src_ref=rows.at[0, :, pl.ds(0, D)],
            dst_ref=rows.at[k, :, pl.ds(0, D)],
            send_sem=send1.at[k],
            recv_sem=recv1.at[k],
            device_id=device(-MARKS[k]),
            device_id_type=MESH,
        )
        copy.start()
        gather.append(copy)

    load_ids.wait()
    total_rows = COUNT * BLK
    lane = lax.broadcasted_iota(jnp.int32, (BLK, total_rows), 1)
    sub = lax.broadcasted_iota(jnp.int32, (BLK, total_rows), 0)
    ids = [cluster[block_at(s)] for s in MARKS]
    bits = pair_bits()
    lane_id = jnp.full((BLK, total_rows), ids[0], jnp.int32)
    lane_bits = jnp.full((BLK, total_rows), bits[0], jnp.int32)
    for l in range(1, COUNT):
        later = lane >= l * BLK
        lane_id = jnp.where(later, ids[l], lane_id)
        lane_bits = jnp.where(later, bits[l], lane_bits)

    for copy in gather:
        copy.wait_recv()

    keys = rows[...].reshape(total_rows, WIDTH)
    scores = lax.dot_general(
        keys[:, :D], keys[:, :D], (((1,), (1,)), ((), ())), preferred_element_type=jnp.float32
    )
    tiles = []
    for k in range(COUNT):
        keep = (lane_id == ids[k]) & ((lane_bits & (1 << k)) != 0)
        if k == 0:
            keep = keep & (lane != sub)
        weights = jnp.exp(scores[k * BLK : (k + 1) * BLK] * (1.0 / (SPREAD * math.sqrt(D))))
        tiles.append(jnp.where(keep, weights, 0.0).astype(jnp.bfloat16))
    sums = jnp.dot(jnp.concatenate(tiles, axis=0), keys, preferred_element_type=jnp.float32)

    back = []
    for k in range(1, COUNT):
        parts[k] = sums[k * BLK : (k + 1) * BLK].astype(jnp.bfloat16)
        copy = pltpu.make_async_remote_copy(
            src_ref=parts.at[k],
            dst_ref=got.at[k],
            send_sem=send2.at[k],
            recv_sem=recv2.at[k],
            device_id=device(MARKS[k]),
            device_id_type=MESH,
        )
        copy.start()
        back.append(copy)

    for copy in gather:
        copy.wait_send()
    own = sums[:BLK]
    for copy in back:
        copy.wait_recv()
    for k in range(1, COUNT):
        own = own + got[k].astype(jnp.float32)
    inverse = 1.0 / own[:, D:]
    for c in range(D // LANES):
        out_ref[:, c * LANES : (c + 1) * LANES] = own[:, c * LANES : (c + 1) * LANES] * inverse
    for copy in back:
        copy.wait_send()


def on_device(embeddings, cluster):
    return pl.pallas_call(
        kernel,
        out_shape=jax.ShapeDtypeStruct((BLK, D), jnp.float32),
        in_specs=[pl.BlockSpec(memory_space=pl.ANY), pl.BlockSpec(memory_space=pl.ANY)],
        out_specs=pl.BlockSpec(memory_space=pltpu.VMEM),
        scratch_shapes=[
            pltpu.VMEM((BLK, D), jnp.bfloat16),
            pltpu.SMEM((BLOCKS,), jnp.int32),
            pltpu.VMEM((COUNT, BLK, WIDTH), jnp.bfloat16),
            pltpu.VMEM((COUNT, BLK, WIDTH), jnp.bfloat16),
            pltpu.VMEM((COUNT, BLK, WIDTH), jnp.bfloat16),
            pltpu.SemaphoreType.DMA((2,)),
            pltpu.SemaphoreType.DMA((COUNT,)),
            pltpu.SemaphoreType.DMA((COUNT,)),
            pltpu.SemaphoreType.DMA((COUNT,)),
            pltpu.SemaphoreType.DMA((COUNT,)),
        ],
        compiler_params=pltpu.CompilerParams(
            collective_id=0, has_side_effects=True, vmem_limit_bytes=32 * 1024 * 1024
        ),
        name="shift",
    )(embeddings, cluster)


def solution(mesh):
    in_specs = (P(("wide", "narrow"), None), P())
    out_specs = P(("wide", "narrow"), None)
    return jax.shard_map(
        on_device, mesh=mesh, in_specs=in_specs, out_specs=out_specs, check_vma=False
    )
```

time: 335 us -> 36.6 us (0.11)
  the two profiles are of different devices: /device:TPU:1 before, /device:TPU:6 now
where the time goes in v1:
time: 36.6 us; the launch traced here: 36.4 us
  Pallas kernels  34.3 us (94%)
  local copies, waits for them, and re-layouts  2.12 us (6%)
    pallas_call x1, Pallas kernels, on_device(): pl.pallas_call(kernel, out_shape=jax.ShapeDtypeStruct((BLK, D), jnp.float...  34.3 us
    unnamed x5, local copies, waits for them, and re-layouts  2.12 us

profile of v1, /device:TPU:6, one launch (start us, length us, event | category | flops | bytes accessed | tf_op | source)
XLA Modules:
  0.0 36.4 jit_solution(4486560904792501483)
XLA Ops:
  0.0 0.0 copy-start
  0.0 0.8 %copy-done = bf16[24,1024]{1,0:T(8,128)(2,1)S(1)} copy-done((bf16[24,1024]{1,0:T(8,128)(2,1)S(1)}, bf16[24,1024]{1,0:T(8,128)(2,1)}, u32[]{:S(2)}) %copy-start) | copy-done | bytes 49176
  0.8 0.0 copy-start.1
  0.8 0.7 %copy-done.1 = s32[512]{0:T(512)S(1)} copy-done((s32[512]{0:T(512)S(1)}, s32[512]{0:T(512)}, u32[]{:S(2)}) %copy-start.1) | copy-done | bytes 2072
  1.5 34.3 %shift.1 = f32[24,1024]{1,0:T(8,128)S(1)} custom-call(bf16[24,1024]{1,0:T(8,128)(2,1)S(1)} %copy-done, s32[512]{0:T(512)S(1)} %copy-done.1), custom_call_target="tpu_custom_call" | custom-call | tf_op jit(solution)/shard_map/shift/pallas_call | solution.py:137
  35.7 0.6 %copy.4 = f32[24,1024]{1,0:T(8,128)} copy(f32[24,1024]{1,0:T(8,128)S(1)} %shift.1) | data formatting | bytes 196608
Async XLA Ops:
  0.0 0.8 %copy-start = (bf16[24,1024]{1,0:T(8,128)(2,1)S(1)}, bf16[24,1024]{1,0:T(8,128)(2,1)}, u32[]{:S(2)}) copy-start(bf16[24,1024]{1,0:T(8,128)(2,1)} %x_hbm.1) | copy-start | bytes 147460
  0.8 0.7 %copy-start.1 = (s32[512]{0:T(512)S(1)}, s32[512]{0:T(512)}, u32[]{:S(2)}) copy-start(s32[512]{0:T(512)} %cluster_hbm.1) | copy-start | bytes 6148

commit v2 on v1

--- a/solution.py
+++ b/solution.py
@@ -16,7 +16,7 @@
 LANES = 128
 MESH = pl.DeviceIdType.MESH
 
-MARKS = (0, 27, 30, 29, 24, 12, 8, -2, -1, 1, 32)
+MARKS = (0, 4, 13, 21, -28, -3, -2, 31, -1, 1, 32)
 COUNT = len(MARKS)
 WIDTH = D + LANES
 
@@ -116,8 +116,15 @@
             device_id=device(MARKS[k]),
             device_id_type=MESH,
         )
-        copy.start()
         back.append(copy)
+    for low, high in ((0, 2), (2, 4), (4, 8)):
+        for k in range(1, COUNT):
+            z = lax.rem(lax.div(block_at(MARKS[k]), 4), 8)
+
+            @pl.when((z >= low) & (z < high))
+            def _():
+                back[k - 1].start()
+
 
     for copy in gather:
         copy.wait_send()
@@ -137,7 +144,7 @@
     return pl.pallas_call(
         kernel,
         out_shape=jax.ShapeDtypeStruct((BLK, D), jnp.float32),
-        in_specs=[pl.BlockSpec(memory_space=pl.ANY), pl.BlockSpec(memory_space=pl.ANY)],
+        in_specs=[pl.BlockSpec(memory_space=pltpu.HBM), pl.BlockSpec(memory_space=pltpu.HBM)],
         out_specs=pl.BlockSpec(memory_space=pltpu.VMEM),
         scratch_shapes=[
             pltpu.VMEM((BLK, D), jnp.bfloat16),
@@ -155,7 +162,7 @@
             collective_id=0, has_side_effects=True, vmem_limit_bytes=32 * 1024 * 1024
         ),
         name="shift",
-    )(embeddings, cluster)
+    )(pltpu.with_memory_space_constraint(embeddings, pltpu.HBM), pltpu.with_memory_space_constraint(cluster, pltpu.HBM))
 
 
 def solution(mesh):

time: 36.6 us -> 33.4 us (0.913)
  the two profiles are of different devices: /device:TPU:6 before, /device:TPU:3 now
where the time goes in v2:
time: 33.4 us; the launch traced here: 33.3 us
  Pallas kernels  32.6 us (98%)
  local copies, waits for them, and re-layouts  0.64 us (2%)
    pallas_call x1, Pallas kernels, on_device(): pl.pallas_call(kernel, out_shape=jax.ShapeDtypeStruct((BLK, D), jnp.float...  32.6 us

profile of v2, /device:TPU:3, one launch (start us, length us, event | category | flops | bytes accessed | tf_op | source)
XLA Modules:
  0.0 33.3 jit_solution(11967377076473643804)
XLA Ops:
  0.0 32.6 %shift.1 = f32[24,1024]{1,0:T(8,128)S(1)} custom-call(bf16[24,1024]{1,0:T(8,128)(2,1)} %x_hbm.1, s32[512]{0:T(512)} %cluster_hbm.1), custom_call_target="tpu_custom_call" | custom-call | tf_op jit(solution)/shard_map/shift/pallas_call | solution.py:144
  32.6 0.6 %copy.4 = f32[24,1024]{1,0:T(8,128)} copy(f32[24,1024]{1,0:T(8,128)S(1)} %shift.1) | data formatting | bytes 196608

commit v3 on v2

--- a/solution.py
+++ b/solution.py
@@ -16,23 +16,37 @@
 LANES = 128
 MESH = pl.DeviceIdType.MESH
 
-MARKS = (0, 4, 13, 21, -28, -3, -2, 31, -1, 1, 32)
+ROW = 4
+GROUPS = BLOCKS // ROW
+MARKS = ((0, 0), (-6, 1), (3, 0), (-2, 3), (7, 3), (0, 2), (-1, 3), (0, 3), (0, 1), (-1, 0), (8, 0))
 COUNT = len(MARKS)
 WIDTH = D + LANES
 
 
-def pair_bits():
+def slots(a, b):
+    return next(
+        (k, l)
+        for k in range(COUNT)
+        for l in range(COUNT)
+        if k != l and MARKS[l][0] - MARKS[k][0] == a and (MARKS[l][1] - MARKS[k][1]) % ROW == b
+    )
+
+
+def pair_bits(place):
+    pairs = [slots(0, 1)]
+    for a in range(1, REACH // ROW + 2):
+        for b in range(ROW):
+            if any(ROW * a + y - x <= REACH for x in range(ROW) for y in range(ROW) if (y - x) % ROW == b):
+                pairs.append(slots(a, b))
     bits = [0] * COUNT
     bits[0] |= 1
-    for gap in range(1, REACH + 1):
-        k, l = next(
-            (k, l)
-            for k in range(COUNT)
-            for l in range(COUNT)
-            if MARKS[l] - MARKS[k] == gap
-        )
+    for k, l in pairs:
         bits[l] |= 1 << k
         bits[k] |= 1 << l
+    k, l = slots(0, 2)
+    low = (place + MARKS[k][1]) % ROW < ROW // 2
+    bits[l] = bits[l] + jnp.where(low, 1 << k, 0)
+    bits[k] = bits[k] + jnp.where(low, 1 << l, 0)
     return bits
 
 
@@ -40,12 +54,13 @@
     n_narrow = lax.axis_size("narrow")
     me = lax.axis_index("wide") * n_narrow + lax.axis_index("narrow")
 
-    def block_at(offset):
-        return lax.rem(me + (offset % BLOCKS), BLOCKS)
+    def block_at(mark, way=1):
+        group = (me // ROW + way * mark[0] + GROUPS) % GROUPS
+        return group * ROW + (me + way * mark[1] + ROW) % ROW
 
-    def device(offset):
-        block = block_at(offset)
-        return (lax.div(block, n_narrow), lax.rem(block, n_narrow))
+    def device(mark, way=1):
+        block = block_at(mark, way)
+        return (block // n_narrow, block % n_narrow)
 
     load = pltpu.make_async_copy(x_hbm, raw, in_sem.at[0])
     load.start()
@@ -70,7 +85,7 @@
             dst_ref=rows.at[k, :, pl.ds(0, D)],
             send_sem=send1.at[k],
             recv_sem=recv1.at[k],
-            device_id=device(-MARKS[k]),
+            device_id=device(MARKS[k], -1),
             device_id_type=MESH,
         )
         copy.start()
@@ -81,7 +96,7 @@
     lane = lax.broadcasted_iota(jnp.int32, (BLK, total_rows), 1)
     sub = lax.broadcasted_iota(jnp.int32, (BLK, total_rows), 0)
     ids = [cluster[block_at(s)] for s in MARKS]
-    bits = pair_bits()
+    bits = pair_bits(me % ROW)
     lane_id = jnp.full((BLK, total_rows), ids[0], jnp.int32)
     lane_bits = jnp.full((BLK, total_rows), bits[0], jnp.int32)
     for l in range(1, COUNT):
@@ -119,7 +134,7 @@
         back.append(copy)
     for low, high in ((0, 2), (2, 4), (4, 8)):
         for k in range(1, COUNT):
-            z = lax.rem(lax.div(block_at(MARKS[k]), 4), 8)
+            z = block_at(MARKS[k]) % n_narrow // ROW
 
             @pl.when((z >= low) & (z < high))
             def _():

time: 33.4 us -> 30.4 us (0.910)
  the two profiles are of different devices: /device:TPU:3 before, /device:TPU:1 now
where the time goes in v3:
time: 30.4 us; the launch traced here: 30.3 us
  Pallas kernels  29.6 us (97%)
  local copies, waits for them, and re-layouts  0.64 us (2%)
    pallas_call x1, Pallas kernels, on_device(): pl.pallas_call(kernel, out_shape=jax.ShapeDtypeStruct((BLK, D), jnp.float...  29.6 us
    unnamed x1, local copies, waits for them, and re-layouts  0.64 us

profile of v3, /device:TPU:1, one launch (start us, length us, event | category | flops | bytes accessed | tf_op | source)
XLA Modules:
  0.0 30.3 jit_solution(2547719141115225535)
XLA Ops:
  0.0 29.6 %shift.1 = f32[24,1024]{1,0:T(8,128)S(1)} custom-call(bf16[24,1024]{1,0:T(8,128)(2,1)} %x_hbm.1, s32[512]{0:T(512)} %cluster_hbm.1), custom_call_target="tpu_custom_call" | custom-call | tf_op jit(solution)/shard_map/shift/pallas_call | solution.py:159
  29.6 0.6 %copy.4 = f32[24,1024]{1,0:T(8,128)} copy(f32[24,1024]{1,0:T(8,128)S(1)} %shift.1) | data formatting | bytes 196608

commit v4 on v3

--- a/solution.py
+++ b/solution.py
@@ -20,7 +20,9 @@
 GROUPS = BLOCKS // ROW
 MARKS = ((0, 0), (-6, 1), (3, 0), (-2, 3), (7, 3), (0, 2), (-1, 3), (0, 3), (0, 1), (-1, 0), (8, 0))
 COUNT = len(MARKS)
-WIDTH = D + LANES
+SUBLANES = 8
+ROW_TILES, LANE_TILES = BLK // SUBLANES, D // LANES
+TILES = ROW_TILES * LANE_TILES + 1
 
 
 def slots(a, b):
@@ -74,15 +76,14 @@
     load.wait()
     values = raw[...].astype(jnp.float32)
     factor = lax.rsqrt(jnp.mean(values * values, axis=1, keepdims=True) + 1e-06)
-    rows[0, :, :D] = (values * factor).astype(jnp.bfloat16)
-    rows[:, :, D:] = jnp.ones((COUNT, BLK, LANES), jnp.bfloat16)
+    rows[0] = (values * factor).astype(jnp.bfloat16)
 
     pl.semaphore_wait(barrier, COUNT - 1)
     gather = []
     for k in range(1, COUNT):
         copy = pltpu.make_async_remote_copy(
-            src_ref=rows.at[0, :, pl.ds(0, D)],
-            dst_ref=rows.at[k, :, pl.ds(0, D)],
+            src_ref=rows.at[0],
+            dst_ref=rows.at[k],
             send_sem=send1.at[k],
             recv_sem=recv1.at[k],
             device_id=device(MARKS[k], -1),
@@ -107,50 +108,70 @@
     for copy in gather:
         copy.wait_recv()
 
-    keys = rows[...].reshape(total_rows, WIDTH)
-    scores = lax.dot_general(
-        keys[:, :D], keys[:, :D], (((1,), (1,)), ((), ())), preferred_element_type=jnp.float32
-    )
-    tiles = []
-    for k in range(COUNT):
-        keep = (lane_id == ids[k]) & ((lane_bits & (1 << k)) != 0)
-        if k == 0:
-            keep = keep & (lane != sub)
-        weights = jnp.exp(scores[k * BLK : (k + 1) * BLK] * (1.0 / (SPREAD * math.sqrt(D))))
-        tiles.append(jnp.where(keep, weights, 0.0).astype(jnp.bfloat16))
-    sums = jnp.dot(jnp.concatenate(tiles, axis=0), keys, preferred_element_type=jnp.float32)
+    keys = rows[...].reshape(total_rows, D)
+    column = lax.broadcasted_iota(jnp.int32, (SUBLANES, LANES), 1)
+    ones = jnp.ones((total_rows, LANES), jnp.bfloat16)
+
+    def partials(first, last):
+        scores = lax.dot_general(
+            keys[first * BLK : last * BLK],
+            keys,
+            (((1,), (1,)), ((), ())),
+            preferred_element_type=jnp.float32,
+        )
+        tiles = []
+        for k in range(first, last):
+            keep = (lane_id == ids[k]) & ((lane_bits & (1 << k)) != 0)
+            if k == 0:
+                keep = keep & (lane != sub)
+            at = (k - first) * BLK
+            weights = jnp.exp(scores[at : at + BLK] * (1.0 / (SPREAD * math.sqrt(D))))
+            tiles.append(jnp.where(keep, weights, 0.0).astype(jnp.bfloat16))
+        rounded = jnp.concatenate(tiles, axis=0)
+        sums = jnp.dot(rounded, keys, preferred_element_type=jnp.float32)
+        totals = jnp.dot(rounded, ones, preferred_element_type=jnp.float32)
+        found = []
+        for k in range(first, last):
+            starts = [(k - first) * BLK + SUBLANES * r for r in range(ROW_TILES)]
+            total = totals[starts[0] : starts[0] + SUBLANES]
+            for r in range(1, ROW_TILES):
+                total = jnp.where(column == r, totals[starts[r] : starts[r] + SUBLANES], total)
+            numerator = [
+                sums[at : at + SUBLANES, c * LANES : (c + 1) * LANES]
+                for at in starts
+                for c in range(LANE_TILES)
+            ]
+            found.append(numerator + [total])
+        return found
 
     back = []
-    for k in range(1, COUNT):
-        parts[k] = sums[k * BLK : (k + 1) * BLK].astype(jnp.bfloat16)
-        copy = pltpu.make_async_remote_copy(
-            src_ref=parts.at[k],
-            dst_ref=got.at[k],
-            send_sem=send2.at[k],
-            recv_sem=recv2.at[k],
-            device_id=device(MARKS[k]),
-            device_id_type=MESH,
-        )
-        back.append(copy)
-    for low, high in ((0, 2), (2, 4), (4, 8)):
-        for k in range(1, COUNT):
-            z = block_at(MARKS[k]) % n_narrow // ROW
-
-            @pl.when((z >= low) & (z < high))
-            def _():
-                back[k - 1].start()
-
+    for first, last in ((1, 6), (6, COUNT)):
+        for k, found in enumerate(partials(first, last), first):
+            for t, tile in enumerate(found):
+                parts[k, t] = tile.astype(jnp.bfloat16)
+            copy = pltpu.make_async_remote_copy(
+                src_ref=parts.at[k],
+                dst_ref=got.at[k],
+                send_sem=send2.at[k],
+                recv_sem=recv2.at[k],
+                device_id=device(MARKS[k]),
+                device_id_type=MESH,
+            )
+            copy.start()
+            back.append(copy)
+    own = partials(0, 1)[0]
 
     for copy in gather:
         copy.wait_send()
-    own = sums[:BLK]
-    for copy in back:
-        copy.wait_recv()
-    for k in range(1, COUNT):
-        own = own + got[k].astype(jnp.float32)
-    inverse = 1.0 / own[:, D:]
-    for c in range(D // LANES):
-        out_ref[:, c * LANES : (c + 1) * LANES] = own[:, c * LANES : (c + 1) * LANES] * inverse
+    for k in reversed(range(1, COUNT)):
+        back[k - 1].wait_recv()
+        own = [tile + got[k, t].astype(jnp.float32) for t, tile in enumerate(own)]
+    inverse = 1.0 / own[-1]
+    for r in range(ROW_TILES):
+        for c in range(LANE_TILES):
+            out_ref[r * SUBLANES : (r + 1) * SUBLANES, c * LANES : (c + 1) * LANES] = (
+                own[r * LANE_TILES + c] * inverse[:, r : r + 1]
+            )
     for copy in back:
         copy.wait_send()
 
@@ -164,9 +185,9 @@
         scratch_shapes=[
             pltpu.VMEM((BLK, D), jnp.bfloat16),
             pltpu.SMEM((BLOCKS,), jnp.int32),
-            pltpu.VMEM((COUNT, BLK, WIDTH), jnp.bfloat16),
-            pltpu.VMEM((COUNT, BLK, WIDTH), jnp.bfloat16),
-            pltpu.VMEM((COUNT, BLK, WIDTH), jnp.bfloat16),
+            pltpu.VMEM((COUNT, BLK, D), jnp.bfloat16),
+            pltpu.VMEM((COUNT, TILES, SUBLANES, LANES), jnp.bfloat16),
+            pltpu.VMEM((COUNT, TILES, SUBLANES, LANES), jnp.bfloat16),
             pltpu.SemaphoreType.DMA((2,)),
             pltpu.SemaphoreType.DMA((COUNT,)),
             pltpu.SemaphoreType.DMA((COUNT,)),

time: 30.4 us -> 29.8 us (0.980)
  Pallas kernels: 29.6 us -> 28.9 us
    pallas_call x1, Pallas kernels: 29.6 us -> 28.9 us  [on_device(): pl.pallas_call(kernel, out_shape=jax.ShapeDtypeStruct((BLK, D), jnp.float...]
where the time goes in v4:
time: 29.8 us; the launch traced here: 29.6 us
  Pallas kernels  28.9 us (97%)
  local copies, waits for them, and re-layouts  0.64 us (2%)
    pallas_call x1, Pallas kernels, on_device(): pl.pallas_call(kernel, out_shape=jax.ShapeDtypeStruct((BLK, D), jnp.float...  28.9 us
    unnamed x1, local copies, waits for them, and re-layouts  0.64 us

profile of v4, /device:TPU:1, one launch (start us, length us, event | category | flops | bytes accessed | tf_op | source)
XLA Modules:
  0.0 29.6 jit_solution(11049232546750930471)
XLA Ops:
  0.0 28.9 %shift.1 = f32[24,1024]{1,0:T(8,128)S(1)} custom-call(bf16[24,1024]{1,0:T(8,128)(2,1)} %x_hbm.1, s32[512]{0:T(512)} %cluster_hbm.1), custom_call_target="tpu_custom_call" | custom-call | tf_op jit(solution)/shard_map/shift/pallas_call | solution.py:180
  29.0 0.6 %copy.4 = f32[24,1024]{1,0:T(8,128)} copy(f32[24,1024]{1,0:T(8,128)S(1)} %shift.1) | data formatting | bytes 196608

commit v5 on v4

--- a/solution.py
+++ b/solution.py
@@ -64,14 +64,14 @@
         block = block_at(mark, way)
         return (block // n_narrow, block % n_narrow)
 
+    barrier = pltpu.get_barrier_semaphore()
+    for k in range(1, COUNT):
+        pl.semaphore_signal(barrier, inc=1, device_id=device(MARKS[k]), device_id_type=MESH)
+
     load = pltpu.make_async_copy(x_hbm, raw, in_sem.at[0])
     load.start()
     load_ids = pltpu.make_async_copy(cluster_hbm, cluster, in_sem.at[1])
     load_ids.start()
-
-    barrier = pltpu.get_barrier_semaphore()
-    for k in range(1, COUNT):
-        pl.semaphore_signal(barrier, inc=1, device_id=device(MARKS[k]), device_id_type=MESH)
 
     load.wait()
     values = raw[...].astype(jnp.float32)
@@ -145,7 +145,7 @@
         return found
 
     back = []
-    for first, last in ((1, 6), (6, COUNT)):
+    for first, last in ((1, 8), (8, COUNT)):
         for k, found in enumerate(partials(first, last), first):
             for t, tile in enumerate(found):
                 parts[k, t] = tile.astype(jnp.bfloat16)

time: 29.8 us -> 29.8 us (level)
  no operation moved by 1% of the time
where the time goes in v5:
time: 29.8 us; the launch traced here: 29.6 us
  Pallas kernels  29 us (97%)
  local copies, waits for them, and re-layouts  0.64 us (2%)
    pallas_call x1, Pallas kernels, on_device(): pl.pallas_call(kernel, out_shape=jax.ShapeDtypeStruct((BLK, D), jnp.float...  29 us
    unnamed x1, local copies, waits for them, and re-layouts  0.64 us

profile of v5, /device:TPU:1, one launch (start us, length us, event | category | flops | bytes accessed | tf_op | source)
XLA Modules:
  0.0 29.6 jit_solution(14177933661791076775)
XLA Ops:
  0.0 29.0 %shift.1 = f32[24,1024]{1,0:T(8,128)S(1)} custom-call(bf16[24,1024]{1,0:T(8,128)(2,1)} %x_hbm.1, s32[512]{0:T(512)} %cluster_hbm.1), custom_call_target="tpu_custom_call" | custom-call | tf_op jit(solution)/shard_map/shift/pallas_call | solution.py:180
  29.0 0.6 %copy.4 = f32[24,1024]{1,0:T(8,128)} copy(f32[24,1024]{1,0:T(8,128)S(1)} %shift.1) | data formatting | bytes 196608
